TPU v7x, 128 devices: a whole 4x4x4 slice. The times are simulated.
128 devices in a mesh: batch: 16 (over y, z), head: 8 (over x, core).
Axes of the slice: x: 4, y: 4, z: 4, core: 2. Of those that a mesh axis runs over, the one named last changes fastest.
Arguments:
- hidden_in: bfloat16 [1024, 3, 2048], P(('batch', 'head')), may hold values from -6 to 6
- states: float32 [1024, 16, 128, 128], P('batch', 'head'), may hold values from -0.8 to 0.8
- norm_in: float32 [2048], replicated, may hold values from 0.1 to 1.9
- w_qk: bfloat16 [2048, 8, 2, 128], P(None, 'head'), may hold values from -0.125 to 0.125
- w_vz: bfloat16 [2048, 16, 2, 128], P(None, 'head'), may hold values from -0.125 to 0.125
- w_ba: bfloat16 [2048, 2, 16], P(None, None, 'head'), may hold values from -0.125 to 0.125
- a_log: float32 [16], P('head'), may hold values from -4 to 1.5
- dt_bias: float32 [16], P('head'), may hold values from -2 to 1
- norm_gate: float32 [128], replicated, may hold values from 0.1 to 1.9
- w_out: bfloat16 [16, 128, 2048], P('head'), may hold values from -0.125 to 0.125
- norm_post: float32 [2048], replicated, may hold values from 0.1 to 1.9
- shared_in: bfloat16 [2048, 2, 512], P('head'), may hold values from -0.125 to 0.125
- shared_gate: bfloat16 [2048], P('head'), may hold values from -0.125 to 0.125
- shared_out: bfloat16 [512, 2048], P(None, 'head'), may hold values from -0.25 to 0.25
- expert_in: bfloat16 [256, 2048, 2, 512], P(('batch', 'head')), may hold values from -0.125 to 0.125
- expert_out: bfloat16 [256, 512, 2048], P(('batch', 'head')), may hold values from -0.25 to 0.25
- routes: int32 [1024, 3, 10], P(('batch', 'head')), may hold values from 0 to 255, all different within a row; in each aligned block of 24 rows (0 to 23, 24 to 47, ..., all dimensions but the last counted through in order) at most 2 rows name the same one
- route_weight: float32 [1024, 3, 10], P(('batch', 'head')), may hold values from 0.02 to 0.25
Outputs:
- layer_out: bfloat16 [1024, 3, 2048], P('batch', None, 'head')
Inputs may be any that keep to these rules, and one draw needn't show every extreme that they name: `routes`: among the 240 choices of one device's tokens, no expert is named more than 2 times, a bound that some block reaches; a token's 10 experts differ.
All inputs are finite; a program needn't handle non-finite values.
Results may differ from a plain program's by a relative error of at most 0.009.
Values may be sent and summed in bfloat16 or wider, within the bound.
A program may use at most 128 MiB of HBM per device.

v0:
```python
import jax
import jax.numpy as jnp
from jax import lax
from jax.experimental import pallas as pl
from jax.experimental.pallas import tpu as pltpu
from jax.sharding import PartitionSpec as P

EPS = 1e-06
MESH = pl.DeviceIdType.MESH
HEADS = 8
BATCH = 16
DEVS = HEADS * BATCH
F32 = jnp.float32
BF16 = jnp.bfloat16
VMEM = pl.BlockSpec(memory_space=pltpu.VMEM)
ANY = pl.BlockSpec(memory_space=pl.ANY)


def rms_scale(values, gain):
    return values * lax.rsqrt(jnp.mean(values * values, axis=-1, keepdims=True) + EPS) * gain


def unit_norm(v):
    return v * lax.rsqrt(jnp.sum(v * v, axis=-1, keepdims=True) + EPS)


def silu(v):
    return v * jax.nn.sigmoid(v)


def iota(shape, axis):
    return lax.broadcasted_iota(jnp.int32, shape, axis)


def mm(left, right):
    return jnp.dot(left, right, preferred_element_type=F32)


def one_hot(mask):
    return jnp.where(mask, 1.0, 0.0)


def spot(p):
    return (p // HEADS, p % HEADS)


def remote(src, dst, send_sem, recv_sem, to):
    return pltpu.make_async_remote_copy(
        src_ref=src, dst_ref=dst, send_sem=send_sem, recv_sem=recv_sem, device_id=to, device_id_type=MESH
    )


def wait_bytes(ref, sem):
    pltpu.make_async_copy(ref, ref, sem).wait()


def take(ref, sem):
    wait_bytes(ref.at[pl.ds(0, ref.shape[0] - 1)], sem)


def spread(p, first, send, recv, send_sem, recv_sem):
    @pl.loop(0, 16)
    def _(i):
        to = first + i

        @pl.when(to != p)
        def _():
            remote(send.at[to], recv.at[p], send_sem, recv_sem, spot(to)).start()

        @pl.when(to == p)
        def _():
            pltpu.make_async_copy(send.at[to], recv.at[p], recv_sem).start()


def part_rows(raw, wide, kinds, lane_of, blocks, from_row=0, to_row=0):
    count = 256 // kinds
    order = one_hot(iota((256, 256), 1) == (iota((256, 256), 0) % count) * kinds + iota((256, 256), 0) // count)
    order = order.astype(BF16)

    @pl.loop(0, blocks)
    def _(i):
        at = pl.multiple_of(from_row + i * 512, 512)
        to = pl.multiple_of(to_row + i * 2 * count, 2 * count)
        pair = jnp.concatenate([raw[pl.ds(at, 256)], raw[pl.ds(at + 256, 256)]], axis=1)
        got = mm(order, pair).astype(BF16)
        for s in range(kinds):
            lane = lane_of(s)
            part = got[count * s : count * s + count]
            wide[pl.ds(to, count), lane : lane + 128] = part[:, :128]
            wide[pl.ds(to + count, count), lane : lane + 128] = part[:, 128:]


def gate_up_lane(s):
    return (s % 2) * 512 + (s // 2) * 128


def count_hits(ids, here):
    hot = jnp.zeros(here.shape, F32)
    for k in range(10):
        hot = hot + one_hot(ids[:, k : k + 1] == here)
    return hot


def delta_rows(rows, ba, rates, gain, states):
    q = unit_norm(silu(rows[:, :128])) * (128 ** -0.5)
    k = unit_norm(silu(rows[:, 128:256]))
    left = jnp.concatenate([k, q], axis=0)
    place = iota((48, 128), 0) % 8
    left = jnp.concatenate([jnp.where(place == s, left, 0.0) for s in range(8)], axis=1)
    right = jnp.concatenate(
        [states[:, 0].reshape(1024, 128), states[:, 1].reshape(1024, 128)], axis=1
    ).astype(BF16)
    met = mm(left.astype(BF16), right)
    q = [q[8 * t : 8 * t + 8] for t in range(3)]
    k = [k[8 * t : 8 * t + 8] for t in range(3)]

    def along(u, v):
        return jnp.sum(u * v, axis=-1, keepdims=True)

    kk = {(i, t): along(k[i], k[t]) for i in range(3) for t in range(i + 1, 3)}
    kq = {(i, t): along(k[i], q[t]) for i in range(3) for t in range(i, 3)}
    heads = []
    for j in range(2):
        lane = slice(128 * j, 128 * j + 128)
        values = silu(rows[:, 256 + 256 * j : 384 + 256 * j])
        gate_z = silu(rows[:, 384 + 256 * j : 512 + 256 * j])
        raw = ba[:, 2 + j : 3 + j] + rates[1:2, j : j + 1]
        decays = jnp.exp(-jnp.exp(rates[0:1, j : j + 1]) * jax.nn.softplus(raw))
        betas = jax.nn.sigmoid(ba[:, j : j + 1])
        decay = [decays[8 * t : 8 * t + 8] for t in range(3)]
        deltas, steps = [], []
        for t in range(3):
            whole = decay[0]
            for i in range(1, t + 1):
                whole = whole * decay[i]
            recalled = whole * met[8 * t : 8 * t + 8, lane]
            readout = whole * met[24 + 8 * t : 32 + 8 * t, lane]
            fade = jnp.ones_like(whole)
            for i in range(t - 1, -1, -1):
                fade = fade * decay[i + 1]
                recalled = recalled + (fade * kk[i, t]) * deltas[i]
                readout = readout + (fade * kq[i, t]) * deltas[i]
            deltas.append(betas[8 * t : 8 * t + 8] * (values[8 * t : 8 * t + 8] - recalled))
            readout = readout + kq[t, t] * deltas[t]
            steps.append(rms_scale(readout, gain) * gate_z[8 * t : 8 * t + 8])
        heads.append(jnp.concatenate(steps, axis=0))
    return jnp.concatenate(heads, axis=1)


def layer_kernel(
    hid_ref, ids_ref, wt_ref, gain_in, rates_ref, gain_gate, gain_post, wba_ref, sgate_ref,
    states_hbm, wqk_hbm, wvz_hbm, wo_hbm, sraw_hbm, down_hbm, win_hbm, wout_hbm,
    out_ref,
    hall, nrm, proj, bas, states, wqk, wvz, wide, wo, sraw, swin, down, raw, win, wout,
    ids_all, wts_all, partb, rs, send, recv, psend, slices, stacked, placing, load, xs,
    back, home, sp, sp_recv, mids,
    in_sem, raw_sem, ag_s, ag_r, i_s, i_r, w_s, w_r, rs_s, rs_r, p_s, p_r, d_s, d_r, b_s, b_r, g_s, g_r, m_s, m_r,
):
    b = lax.axis_index("batch")
    h = lax.axis_index("head")
    p = b * HEADS + h
    mine = p // 16
    x, c = h // 2, h % 2
    sib = x * 2 + 1 - c

    def to_heads(src, dst, ssem, rsem):
        for i in range(1, HEADS):
            to = (h + i) % HEADS
            remote(src(to), dst.at[h], ssem, rsem, (b, to)).start()

    loads = [
        pltpu.make_async_copy(src, dst, in_sem.at[n])
        for n, (src, dst) in enumerate(
            [(wqk_hbm, wqk), (wvz_hbm, wvz), (states_hbm, states), (wo_hbm, wo), (sraw_hbm, sraw),
             (down_hbm, down), (wout_hbm, wout)]
        )
    ]
    wqk_in, wvz_in, states_in, wo_in, sraw_in, down_in, wout_in = loads
    for copy in loads:
        copy.start()

    def raw_in(n):
        return pltpu.make_async_copy(
            win_hbm.at[pl.ds(n * 8192, 8192)], raw.at[n % 2], raw_sem.at[n % 2]
        )

    raw_in(0).start()
    raw_in(1).start()

    barrier = pltpu.get_barrier_semaphore()

    @pl.loop(1, DEVS)
    def _(i):
        pl.semaphore_signal(barrier, inc=1, device_id=spot((p + i) % DEVS), device_id_type=MESH)

    wqk_in.wait()
    part_rows(wqk, wide, 2, lambda s: 128 * s, 8)
    pl.semaphore_wait(barrier, DEVS - 1)

    sent = []

    def pass_on(src, slot, to):
        copy = remote(src, hall.at[slot], ag_s.at[len(sent)], ag_r.at[slot], (b, to))
        copy.start()
        sent.append(copy)

    def norm_block(slot):
        rows = rms_scale(hall[slot].astype(F32).reshape(24, 2048), gain_in[...])
        nrm[pl.ds(pl.multiple_of(slot * 24, 8), 24)] = rows

    for d in (1, 3, 2):
        pass_on(hid_ref, h, ((x + d) % 4) * 2 + c)
    pass_on(hid_ref, h, sib)
    to_heads(lambda to: ids_ref, ids_all, i_s, i_r)
    to_heads(lambda to: wt_ref, wts_all, w_s, w_r)
    ids_all[h] = ids_ref[...]
    wts_all[h] = wt_ref[...]
    hall[h] = hid_ref[...]
    norm_block(h)
    wvz_in.wait()
    part_rows(wvz, wide, 4, lambda s: 256 + 128 * s, 16)
    for d in (3, 1, 2):
        slot = ((x + d) % 4) * 2 + c
        wait_bytes(hall.at[slot], ag_r.at[slot])
        pass_on(hall.at[slot], slot, sib)
    for d in (3, 1, 2):
        norm_block(((x + d) % 4) * 2 + c)
    for d in (0, 3, 1, 2):
        slot = ((x + d) % 4) * 2 + 1 - c
        wait_bytes(hall.at[slot], ag_r.at[slot])
        norm_block(slot)

    left = nrm[...].astype(BF16)
    for n in range(3):
        proj[:, 256 * n : 256 * n + 256] = mm(left, wide[:, 256 * n : 256 * n + 256])
    wba = wba_ref[...].astype(F32)
    wba = jnp.concatenate([wba[0], wba[1], jnp.zeros((4, 2048), F32)], axis=0).astype(BF16)
    bas[...] = lax.dot_general(left, wba, (((1,), (1,)), ((), ())), preferred_element_type=F32)

    states_in.wait()
    wo_in.wait()

    @pl.loop(0, HEADS)
    def _(i):
        o = (h + 1 + i) % HEADS
        at = pl.multiple_of(o * 24, 8)
        gated = delta_rows(
            proj[pl.ds(at, 24)], bas[pl.ds(at, 24)], rates_ref[...], gain_gate[...],
            states[pl.ds(pl.multiple_of(o * 8, 8), 8)],
        )
        gated = jnp.concatenate([gated, jnp.zeros((8, 256), F32)], axis=0).astype(BF16)
        partb[o] = mm(gated, wo[...])[:24].astype(BF16).reshape(3, 8, 2048)

        @pl.when(i < HEADS - 1)
        def _():
            remote(partb.at[o], rs.at[h], rs_s, rs_r, (b, o)).start()

    i0, i1 = iota((128, 128), 0), iota((128, 128), 1)
    later = one_hot((i0 // 32 == i1 // 32) & (i1 < i0)).astype(BF16)
    own = jnp.concatenate([ids_ref[...].reshape(24, 10), jnp.full((8, 10), -1, jnp.int32)], axis=0)
    own = jnp.concatenate([own] * 4, axis=0)
    col = iota((128, 256), 1)
    col_chunk, col_rank = (col // 4) % 4, (col % 2).astype(F32)
    named = (col // 16) * 2 + (col // 2) % 2
    row_chunk = iota((128, 256), 0) // 32

    @pl.loop(0, 8)
    def _(g):
        hot = count_hits(own, named + g * 32)
        before = mm(later, hot.astype(BF16))
        chosen = jnp.where((before == col_rank) & (row_chunk == col_chunk), hot, 0.0)
        placing[g] = chosen.T.astype(BF16)

    sraw_in.wait()
    part_rows(sraw, swin, 8, gate_up_lane, 4)

    take(rs, rs_r)
    total = partb[h].astype(F32)
    for i in range(1, HEADS):
        total = total + rs[(h + i) % HEADS].astype(F32)
    resid = (hid_ref[...].astype(F32) + total).astype(BF16)
    post = rms_scale(resid.astype(F32), gain_post[...].reshape(1, 1, 2048)).astype(BF16)
    rows = post.astype(F32).reshape(24, 2048)
    blank = jnp.zeros((8, 512), F32)
    stacked[...] = jnp.concatenate(
        [v for j in range(4) for v in (rows[:, 512 * j : 512 * j + 512], blank)], axis=0
    ).astype(BF16)
    for i in range(HEADS):
        psend[i, 0] = resid[:, :, 256 * i : 256 * i + 256]
        psend[i, 1] = post[:, :, 256 * i : 256 * i + 256]
    to_heads(lambda to: psend.at[to], slices, p_s, p_r)
    slices[h] = psend[h]

    @pl.loop(0, 8)
    def _(i):
        group = (mine + i) % 8
        rows = mm(placing[group], stacked[...]).astype(BF16)
        send[pl.ds(group * 16, 16)] = rows.reshape(16, 16, 512)
        spread(p, group * 16, send, recv, d_s, d_r.at[mine])

    take(slices, p_r)
    every = slices[:, 1].astype(F32).reshape(192, 256)
    up = mm(every.astype(BF16), swin[...])
    logit = jnp.sum(every * sgate_ref[...].astype(F32), axis=-1, keepdims=True)
    high = logit.astype(BF16).astype(F32)
    zero = jnp.zeros((192, 126), F32)
    sp[...] = (
        jnp.concatenate([up, high, logit - high, zero], axis=1).astype(BF16).reshape(HEADS, 3, 8, 1152)
    )
    to_heads(lambda to: sp.at[to], sp_recv, g_s, g_r)

    for n in range(4):
        raw_in(n).wait()
        part_rows(raw.at[n % 2], win, 8, gate_up_lane, 16, 0, n * 1024)
        if n < 2:
            raw_in(n + 2).start()

    take(ids_all, i_r)
    take(wts_all, w_r)
    ids = ids_all[...].reshape(192, 10)
    wts = wts_all[...].reshape(192, 10)
    i0, i1 = iota((192, 192), 0), iota((192, 192), 1)
    later2 = one_hot((i0 // 24 == i1 // 24) & (i1 < i0)).astype(BF16)
    col2 = iota((192, 512), 1)
    named2 = (col2 // 32) * 2 + (col2 // 16) % 2
    rank2 = ((col2 // 8) % 2).astype(F32)
    kept = iota((192, 512), 0) // 24 == col2 % 8

    @pl.loop(0, 8)
    def _(g):
        here = named2 + g * 32
        hot = jnp.zeros((192, 512), F32)
        heavy = jnp.zeros((192, 512), F32)
        for k in range(10):
            same = ids[:, k : k + 1] == here
            hot = hot + one_hot(same)
            heavy = heavy + jnp.where(same, wts[:, k : k + 1], 0.0)
        before = mm(later2, hot.astype(BF16))
        heavy = jnp.where((before == rank2) & kept, heavy, 0.0)
        top = heavy.astype(BF16)
        load[g, 0] = top
        load[g, 1] = (heavy - top.astype(F32)).astype(BF16)

    source, inside = iota((256, 256), 1) // 16, iota((256, 256), 1) % 16
    target = (inside // 4) * 64 + ((inside // 2) % 2) * 32 + (source // 8) * 16 + (inside % 2) * 8 + source % 8
    order = one_hot(iota((256, 256), 0) == target).astype(BF16)
    wout_in.wait()
    for half in range(2):
        @pl.loop(0, 4)
        def _(i):
            group = (mine + 8 - (4 * half + i)) % 8
            wait_bytes(recv.at[pl.ds(group * 16, 16)], d_r.at[group])
            got = mm(order, recv[pl.ds(group * 16, 16)].reshape(256, 512)).astype(BF16)
            to = pl.multiple_of(i * 32, 32)
            for j in range(4):
                for e in range(2):
                    at = j * 64 + e * 32
                    xs[e, pl.ds(to, 32), 512 * j : 512 * j + 512] = got[at : at + 32]

        @pl.loop(0, 2)
        def _(e):
            inner = []
            for n in range(2):
                lane = slice(256 * n, 256 * n + 256)
                lane2 = slice(512 + 256 * n, 768 + 256 * n)
                gate = mm(xs[e], win[pl.ds(e * 2048, 2048), lane])
                more = mm(xs[e], win[pl.ds(e * 2048, 2048), lane2])
                inner.append((silu(gate) * more).astype(BF16))
            inner = jnp.concatenate(inner, axis=1)
            rows = pl.ds(pl.multiple_of(e * 16, 16), 16)
            for f in range(HEADS):
                got = mm(inner, wout[e, :, 256 * f : 256 * f + 256]).astype(BF16)
                for i in range(4):
                    group = (mine + 8 - (4 * half + i)) % 8
                    for n in range(2):
                        at = 32 * i + 16 * n
                        back[group * 16 + n * 8 + f, rows, :] = got[at : at + 16]

        @pl.loop(0, 4)
        def _(i):
            group = (mine + 8 - (4 * half + i)) % 8
            spread(p, group * 16, back, home, b_s, b_r)

        if half == 0:
            take(sp_recv, g_r)
            total = sp[h].astype(F32)
            for i in range(1, HEADS):
                total = total + sp_recv[(h + i) % HEADS].astype(F32)
            logit = total[:, :, 1024:1025] + total[:, :, 1025:1026]
            mid = silu(total[:, :, :512]) * total[:, :, 512:1024] * jax.nn.sigmoid(logit)
            mids[h] = mid.astype(BF16)
            to_heads(lambda to: mids.at[h], mids, m_s, m_r)

    down_in.wait()
    take(mids, m_r)
    every = mids[...].astype(F32).reshape(192, 512).astype(BF16)
    shared = mm(every, down[...])
    near = slices[:, 0].astype(F32).reshape(192, 256) + shared
    wait_bytes(home, b_r)
    acc = jnp.zeros((192, 256), F32)
    for g in range(8):
        got = home[16 * g : 16 * g + 16].reshape(512, 256)
        acc = acc + mm(load[g, 0], got) + mm(load[g, 1], got)
    out = (near + acc.astype(BF16).astype(F32)).astype(BF16).reshape(HEADS, 3, 8, 256)
    for o in range(HEADS):
        out_ref[:, o] = out[o]
    for copy in sent:
        copy.wait_send()
    take(ids_all, i_s)
    take(wts_all, w_s)
    take(rs, rs_s)
    take(psend, p_s)
    take(send, d_s)
    take(sp, g_s)
    take(mids, m_s)
    take(back, b_s)


def layer(*args):
    dma = pltpu.SemaphoreType.DMA
    return pl.pallas_call(
        layer_kernel,
        name="layer",
        out_shape=jax.ShapeDtypeStruct((3, HEADS, 8, 256), BF16),
        in_specs=[VMEM] * 9 + [ANY] * 8,
        out_specs=VMEM,
        scratch_shapes=[
            pltpu.VMEM((HEADS, 3, 8, 2048), BF16),
            pltpu.VMEM((192, 2048), F32),
            pltpu.VMEM((192, 768), F32),
            pltpu.VMEM((192, 8), F32),
            pltpu.VMEM((64, 2, 128, 128), F32),
            pltpu.VMEM((4096, 128), BF16),
            pltpu.VMEM((8192, 128), BF16),
            pltpu.VMEM((2048, 768), BF16),
            pltpu.VMEM((256, 2048), BF16),
            pltpu.VMEM((2048, 128), BF16),
            pltpu.VMEM((256, 1024), BF16),
            pltpu.VMEM((512, 256), BF16),
            pltpu.VMEM((2, 8192, 128), BF16),
            pltpu.VMEM((4096, 1024), BF16),
            pltpu.VMEM((2, 512, 2048), BF16),
            pltpu.VMEM((HEADS, 3, 8, 10), jnp.int32),
            pltpu.VMEM((HEADS, 3, 8, 10), F32),
            pltpu.VMEM((HEADS, 3, 8, 2048), BF16),
            pltpu.VMEM((HEADS, 3, 8, 2048), BF16),
            pltpu.VMEM((DEVS, 16, 512), BF16),
            pltpu.VMEM((DEVS, 16, 512), BF16),
            pltpu.VMEM((HEADS, 2, 3, 8, 256), BF16),
            pltpu.VMEM((HEADS, 2, 3, 8, 256), BF16),
            pltpu.VMEM((128, 512), BF16),
            pltpu.VMEM((8, 256, 128), BF16),
            pltpu.VMEM((8, 2, 192, 512), BF16),
            pltpu.VMEM((2, 128, 2048), BF16),
            pltpu.VMEM((DEVS, 32, 256), BF16),
            pltpu.VMEM((DEVS, 32, 256), BF16),
            pltpu.VMEM((HEADS, 3, 8, 1152), BF16),
            pltpu.VMEM((HEADS, 3, 8, 1152), BF16),
            pltpu.VMEM((HEADS, 3, 8, 512), BF16),
            dma((7,)), dma((2,)), dma((7,)), dma((HEADS,)),
        ]
        + [dma(())] * 9
        + [dma((8,))]
        + [dma(())] * 6,
        compiler_params=pltpu.CompilerParams(
            collective_id=0, has_side_effects=True, vmem_limit_bytes=60 * 2**20
        ),
    )(*args)


def column_rows(w):
    return w.reshape(-1, 2, 4, 128).transpose(0, 2, 1, 3).reshape(-1, 128)


def shards(
    hidden_in, states, norm_in, w_qk, w_vz, w_ba, a_log, dt_bias, norm_gate, w_out, norm_post,
    shared_in, shared_gate, shared_out, expert_in, expert_out, routes, route_weight,
):
    out = layer(
        hidden_in.transpose(1, 0, 2),
        routes.transpose(1, 0, 2),
        route_weight.transpose(1, 0, 2),
        norm_in.reshape(1, 2048),
        jnp.stack([a_log, dt_bias]),
        norm_gate.reshape(1, 128),
        norm_post.reshape(1, 2048),
        w_ba.transpose(1, 2, 0),
        shared_gate.reshape(1, 256),
        states,
        w_qk.reshape(4096, 128),
        w_vz.reshape(8192, 128),
        w_out.reshape(256, 2048),
        column_rows(shared_in),
        shared_out,
        column_rows(expert_in),
        expert_out,
    )
    return out.reshape(3, 64, 256).transpose(1, 0, 2)


def solution(mesh):
    in_specs = (
        P(("batch", "head"), None, None),
        P("batch", "head", None, None),
        P(),
        P(None, "head", None, None),
        P(None, "head", None, None),
        P(None, None, "head"),
        P("head"),
        P("head"),
        P(),
        P("head", None, None),
        P(),
        P("head", None, None),
        P("head"),
        P(None, "head"),
        P(("batch", "head"), None, None, None),
        P(("batch", "head"), None, None),
        P(("batch", "head"), None, None),
        P(("batch", "head"), None, None),
    )
    out_specs = P("batch", None, "head")
    return jax.shard_map(shards, mesh=mesh, in_specs=in_specs, out_specs=out_specs, check_vma=False)
```

profile of v0, /device:TPU:1, one launch (start us, length us, event | category | flops | bytes accessed | tf_op | source)
XLA Modules:
  0.0 106.4 jit_solution(11700418634227367223)
XLA Ops:
  0.0 1.2 %pad_maximum_fusion.rates_ref = f32[2,2]{1,0:T(2,128)} fusion(f32[1,2]{1,0:T(1,128)} %bitcast.38, f32[1,2]{1,0:T(1,128)} %bitcast.39), kind=kLoop, calls=%fused_computation | loop fusion | flops 4 | bytes 32 | tf_op jit(solution)/shard_map/stack | solution.py:484
  1.2 1.2 %reshape.39.sgate_ref = bf16[1,256]{1,0:T(2,128)(2,1)} reshape(bf16[256]{0:T(256)(128)(2,1)} %param.30) | data formatting | bytes 1024 | tf_op jit(solution)/shard_map/reshape | solution.py:488
  2.5 102.4 %layer.1 = bf16[3,8,8,256]{3,2,1,0:T(8,128)(2,1)} custom-call(bf16[3,8,2048]{2,1,0:T(8,128)(2,1)} %bitcast.31, s32[3,8,10]{2,1,0:T(8,128)} %bitcast.33, f32[3,8,10]{2,1,0:T(8,128)} %bitcast.34, f32[1,2048]{1,0:T(1,128)} %bitcast.35, f32[2,2]{1,0:T(2,128)} %pad_maximum_fusion.rates_ref, f32[1,128]{1,0:T(1,128)} %bitcast.37, f32[1,2048]{1,0:T(1,128)} %bitcast.36, ...), custom_call_target="tpu_custom_call" | custom-call | tf_op jit(solution)/shard_map/layer/pallas_call | solution.py:421
  104.8 1.5 %copy.22 = bf16[64,3,256]{2,0,1:T(8,128)(2,1)} copy(bf16[64,3,256]{2,0,1:T(8,128)(2,1)} %bitcast.30) | data formatting | bytes 196608
where the time goes:
time: 107 us; the launch traced here: 106 us
  Pallas kernels  102 us (95%)
  local copies, waits for them, and re-layouts  2.78 us (3%)
  other arithmetic  1.24 us (1%)
    pallas_call x1, Pallas kernels, layer(): pl.pallas_call(layer_kernel, name='layer', out_shape=jax.ShapeDtypeStruct...  102 us

commit v1 on v0

--- a/solution.py
+++ b/solution.py
@@ -58,18 +58,17 @@
     wait_bytes(ref.at[pl.ds(0, ref.shape[0] - 1)], sem)
 
 
-def spread(p, first, send, recv, send_sem, recv_sem):
-    @pl.loop(0, 16)
-    def _(i):
-        to = first + i
-
-        @pl.when(to != p)
-        def _():
-            remote(send.at[to], recv.at[p], send_sem, recv_sem, spot(to)).start()
-
-        @pl.when(to == p)
-        def _():
-            pltpu.make_async_copy(send.at[to], recv.at[p], recv_sem).start()
+def plane_offset(place):
+    dy = (place % 8) // 2
+    return dy, (place % 2) * 2 + (dy + place // 8) % 2
+
+
+def far_first(half):
+    def hops(position):
+        dy, dz = plane_offset(position // 8)
+        return sum(min(d, 4 - d) for d in (dy, dz, (position % 8) // 2))
+
+    return sorted(range(64 * half, 64 * half + 64), key=lambda position: (-hops(position), position % 5, position))
 
 
 def part_rows(raw, wide, kinds, lane_of, blocks, from_row=0, to_row=0):
@@ -77,7 +76,7 @@
     order = one_hot(iota((256, 256), 1) == (iota((256, 256), 0) % count) * kinds + iota((256, 256), 0) // count)
     order = order.astype(BF16)
 
-    @pl.loop(0, blocks)
+    @pl.loop(0, blocks, unroll=4)
     def _(i):
         at = pl.multiple_of(from_row + i * 512, 512)
         to = pl.multiple_of(to_row + i * 2 * count, 2 * count)
@@ -124,8 +123,8 @@
         lane = slice(128 * j, 128 * j + 128)
         values = silu(rows[:, 256 + 256 * j : 384 + 256 * j])
         gate_z = silu(rows[:, 384 + 256 * j : 512 + 256 * j])
-        raw = ba[:, 2 + j : 3 + j] + rates[1:2, j : j + 1]
-        decays = jnp.exp(-jnp.exp(rates[0:1, j : j + 1]) * jax.nn.softplus(raw))
+        raw = ba[:, 2 + j : 3 + j] + rates[1][:, j : j + 1]
+        decays = jnp.exp(-jnp.exp(rates[0][:, j : j + 1]) * jax.nn.softplus(raw))
         betas = jax.nn.sigmoid(ba[:, j : j + 1])
         decay = [decays[8 * t : 8 * t + 8] for t in range(3)]
         deltas, steps = [], []
@@ -148,44 +147,51 @@
 
 
 def layer_kernel(
-    hid_ref, ids_ref, wt_ref, gain_in, rates_ref, gain_gate, gain_post, wba_ref, sgate_ref,
+    hid_ref, ids_ref, wt_ref, gain_in, alog_ref, dt_ref, gain_gate, gain_post, wba_ref, sgate_ref,
     states_hbm, wqk_hbm, wvz_hbm, wo_hbm, sraw_hbm, down_hbm, win_hbm, wout_hbm,
     out_ref,
     hall, nrm, proj, bas, states, wqk, wvz, wide, wo, sraw, swin, down, raw, win, wout,
-    ids_all, wts_all, partb, rs, send, recv, psend, slices, stacked, placing, load, xs,
+    ids_all, wts_all, partb, fs, rs, send, recv, psend, slices, stacked, placing, load, xs,
     back, home, sp, sp_recv, mids,
-    in_sem, raw_sem, ag_s, ag_r, i_s, i_r, w_s, w_r, rs_s, rs_r, p_s, p_r, d_s, d_r, b_s, b_r, g_s, g_r, m_s, m_r,
+    in_sem, raw_sem, ag_s, ag_r, i_s, i_r, w_s, w_r, f_s, f_r, rs_s, rs_r, p_s, p_r, d_s, d_r, b_s, b_r, g_s, g_r, m_s, m_r,
 ):
     b = lax.axis_index("batch")
     h = lax.axis_index("head")
     p = b * HEADS + h
-    mine = p // 16
     x, c = h // 2, h % 2
     sib = x * 2 + 1 - c
+    y, z = b // 4, b % 4
+
+    def batch_at(place, sign):
+        dy, dz = plane_offset(place)
+        return ((y + 4 + sign * dy) % 4) * 4 + (z + 4 + sign * dz) % 4
+
+    def head_at(member, sign):
+        return ((x + 4 + sign * (member // 2)) % 4) * 2 + (c + member) % 2
 
     def to_heads(src, dst, ssem, rsem):
         for i in range(1, HEADS):
             to = (h + i) % HEADS
             remote(src(to), dst.at[h], ssem, rsem, (b, to)).start()
 
-    loads = [
-        pltpu.make_async_copy(src, dst, in_sem.at[n])
-        for n, (src, dst) in enumerate(
-            [(wqk_hbm, wqk), (wvz_hbm, wvz), (states_hbm, states), (wo_hbm, wo), (sraw_hbm, sraw),
-             (down_hbm, down), (wout_hbm, wout)]
-        )
+    pairs = [
+        (wqk_hbm, wqk), (wvz_hbm, wvz), (sraw_hbm, sraw), (states_hbm, states), (wo_hbm, wo),
+        (down_hbm, down), (wout_hbm, wout),
     ]
-    wqk_in, wvz_in, states_in, wo_in, sraw_in, down_in, wout_in = loads
-    for copy in loads:
-        copy.start()
+    loads = [pltpu.make_async_copy(src, dst, in_sem.at[n]) for n, (src, dst) in enumerate(pairs)]
+    wqk_in, wvz_in, sraw_in, states_in, wo_in, down_in, wout_in = loads
 
     def raw_in(n):
         return pltpu.make_async_copy(
             win_hbm.at[pl.ds(n * 8192, 8192)], raw.at[n % 2], raw_sem.at[n % 2]
         )
 
+    for copy in loads[:4]:
+        copy.start()
     raw_in(0).start()
     raw_in(1).start()
+    for copy in loads[4:]:
+        copy.start()
 
     barrier = pltpu.get_barrier_semaphore()
 
@@ -193,8 +199,6 @@
     def _(i):
         pl.semaphore_signal(barrier, inc=1, device_id=spot((p + i) % DEVS), device_id_type=MESH)
 
-    wqk_in.wait()
-    part_rows(wqk, wide, 2, lambda s: 128 * s, 8)
     pl.semaphore_wait(barrier, DEVS - 1)
 
     sent = []
@@ -208,7 +212,7 @@
         rows = rms_scale(hall[slot].astype(F32).reshape(24, 2048), gain_in[...])
         nrm[pl.ds(pl.multiple_of(slot * 24, 8), 24)] = rows
 
-    for d in (1, 3, 2):
+    for d in (2, 1, 3):
         pass_on(hid_ref, h, ((x + d) % 4) * 2 + c)
     pass_on(hid_ref, h, sib)
     to_heads(lambda to: ids_ref, ids_all, i_s, i_r)
@@ -217,12 +221,19 @@
     wts_all[h] = wt_ref[...]
     hall[h] = hid_ref[...]
     norm_block(h)
-    wvz_in.wait()
-    part_rows(wvz, wide, 4, lambda s: 256 + 128 * s, 16)
-    for d in (3, 1, 2):
+    wqk_in.wait()
+    part_rows(wqk, wide, 2, lambda s: 128 * s, 8)
+
+    def forward(d):
         slot = ((x + d) % 4) * 2 + c
         wait_bytes(hall.at[slot], ag_r.at[slot])
         pass_on(hall.at[slot], slot, sib)
+
+    forward(3)
+    forward(1)
+    forward(2)
+    wvz_in.wait()
+    part_rows(wvz, wide, 4, lambda s: 256 + 128 * s, 16)
     for d in (3, 1, 2):
         norm_block(((x + d) % 4) * 2 + c)
     for d in (0, 3, 1, 2):
@@ -240,20 +251,32 @@
     states_in.wait()
     wo_in.wait()
 
-    @pl.loop(0, HEADS)
-    def _(i):
-        o = (h + 1 + i) % HEADS
+    def partial_rows(o):
         at = pl.multiple_of(o * 24, 8)
         gated = delta_rows(
-            proj[pl.ds(at, 24)], bas[pl.ds(at, 24)], rates_ref[...], gain_gate[...],
+            proj[pl.ds(at, 24)], bas[pl.ds(at, 24)], (alog_ref[...], dt_ref[...]), gain_gate[...],
             states[pl.ds(pl.multiple_of(o * 8, 8), 8)],
         )
         gated = jnp.concatenate([gated, jnp.zeros((8, 256), F32)], axis=0).astype(BF16)
-        partb[o] = mm(gated, wo[...])[:24].astype(BF16).reshape(3, 8, 2048)
-
-        @pl.when(i < HEADS - 1)
-        def _():
-            remote(partb.at[o], rs.at[h], rs_s, rs_r, (b, o)).start()
+        return mm(gated, wo[...])[:24].reshape(3, 8, 2048)
+
+    @pl.loop(0, 3)
+    def _(k):
+        o = ((x + 1 + k) % 4) * 2 + 1 - c
+        partb[o] = partial_rows(o).astype(BF16)
+        remote(partb.at[o], fs.at[k], f_s, f_r.at[k], (b, sib)).start()
+
+    @pl.loop(0, 3)
+    def _(k):
+        o = ((x + 1 + k) % 4) * 2 + c
+        rows = partial_rows(o)
+        wait_bytes(fs.at[k], f_r.at[k])
+        partb[o] = (rows + fs[k].astype(F32)).astype(BF16)
+        remote(partb.at[o], rs.at[k], rs_s, rs_r, (b, o)).start()
+
+    partb[sib] = partial_rows(sib).astype(BF16)
+    remote(partb.at[sib], rs.at[3], rs_s, rs_r, (b, sib)).start()
+    total = partial_rows(h)
 
     i0, i1 = iota((128, 128), 0), iota((128, 128), 1)
     later = one_hot((i0 // 32 == i1 // 32) & (i1 < i0)).astype(BF16)
@@ -261,12 +284,13 @@
     own = jnp.concatenate([own] * 4, axis=0)
     col = iota((128, 256), 1)
     col_chunk, col_rank = (col // 4) % 4, (col % 2).astype(F32)
-    named = (col // 16) * 2 + (col // 2) % 2
+    named = head_at((col // 16) % 8, 1) * 2 + (col // 2) % 2
     row_chunk = iota((128, 256), 0) // 32
 
     @pl.loop(0, 8)
     def _(g):
-        hot = count_hits(own, named + g * 32)
+        first, second = batch_at(2 * g, 1) * 16, batch_at(2 * g + 1, 1) * 16
+        hot = count_hits(own, named + jnp.where(col < 128, first, second))
         before = mm(later, hot.astype(BF16))
         chosen = jnp.where((before == col_rank) & (row_chunk == col_chunk), hot, 0.0)
         placing[g] = chosen.T.astype(BF16)
@@ -274,10 +298,9 @@
     sraw_in.wait()
     part_rows(sraw, swin, 8, gate_up_lane, 4)
 
-    take(rs, rs_r)
-    total = partb[h].astype(F32)
-    for i in range(1, HEADS):
-        total = total + rs[(h + i) % HEADS].astype(F32)
+    wait_bytes(rs, rs_r)
+    for i in range(4):
+        total = total + rs[i].astype(F32)
     resid = (hid_ref[...].astype(F32) + total).astype(BF16)
     post = rms_scale(resid.astype(F32), gain_post[...].reshape(1, 1, 2048)).astype(BF16)
     rows = post.astype(F32).reshape(24, 2048)
@@ -291,13 +314,27 @@
     to_heads(lambda to: psend.at[to], slices, p_s, p_r)
     slices[h] = psend[h]
 
-    @pl.loop(0, 8)
-    def _(i):
-        group = (mine + i) % 8
-        rows = mm(placing[group], stacked[...]).astype(BF16)
-        send[pl.ds(group * 16, 16)] = rows.reshape(16, 16, 512)
-        spread(p, group * 16, send, recv, d_s, d_r.at[mine])
-
+    for half in range(2):
+        @pl.loop(4 * half, 4 * half + 4)
+        def _(g):
+            rows = mm(placing[g], stacked[...]).astype(BF16)
+            send[pl.ds(g * 16, 16)] = rows.reshape(16, 16, 512)
+
+        for n in far_first(half):
+            if n:
+                to = (batch_at(n // 8, 1), head_at(n % 8, 1))
+                remote(send.at[n], recv.at[n], d_s, d_r.at[half], to).start()
+            else:
+                pltpu.make_async_copy(send.at[n], recv.at[n], d_r.at[half]).start()
+
+    def lay_out(n):
+        raw_in(n).wait()
+        part_rows(raw.at[n % 2], win, 8, gate_up_lane, 16, 0, n * 1024)
+        if n < 2:
+            raw_in(n + 2).start()
+
+    lay_out(0)
+    lay_out(1)
     take(slices, p_r)
     every = slices[:, 1].astype(F32).reshape(192, 256)
     up = mm(every.astype(BF16), swin[...])
@@ -309,11 +346,8 @@
     )
     to_heads(lambda to: sp.at[to], sp_recv, g_s, g_r)
 
-    for n in range(4):
-        raw_in(n).wait()
-        part_rows(raw.at[n % 2], win, 8, gate_up_lane, 16, 0, n * 1024)
-        if n < 2:
-            raw_in(n + 2).start()
+    lay_out(2)
+    lay_out(3)
 
     take(ids_all, i_r)
     take(wts_all, w_r)
@@ -321,36 +355,39 @@
     wts = wts_all[...].reshape(192, 10)
     i0, i1 = iota((192, 192), 0), iota((192, 192), 1)
     later2 = one_hot((i0 // 24 == i1 // 24) & (i1 < i0)).astype(BF16)
-    col2 = iota((192, 512), 1)
-    named2 = (col2 // 32) * 2 + (col2 // 16) % 2
-    rank2 = ((col2 // 8) % 2).astype(F32)
-    kept = iota((192, 512), 0) // 24 == col2 % 8
+    named2 = iota((192, 64), 1) // 2
+    rank2 = (iota((192, 64), 1) % 2).astype(F32)
+    widen = one_hot(iota((64, 512), 1) // 8 == iota((64, 512), 0)).astype(BF16)
+    col2 = iota((384, 512), 1)
+    source_head, member = (col2 // 32) % 8, col2 % 8
+    owner = ((source_head // 2 + 4 - member // 2) % 4) * 2 + (source_head + member) % 2
+    kept = (iota((384, 512), 0) % 192) // 24 == owner
 
     @pl.loop(0, 8)
     def _(g):
         here = named2 + g * 32
-        hot = jnp.zeros((192, 512), F32)
-        heavy = jnp.zeros((192, 512), F32)
+        hot = jnp.zeros((192, 64), F32)
+        heavy = jnp.zeros((192, 64), F32)
         for k in range(10):
             same = ids[:, k : k + 1] == here
             hot = hot + one_hot(same)
             heavy = heavy + jnp.where(same, wts[:, k : k + 1], 0.0)
         before = mm(later2, hot.astype(BF16))
-        heavy = jnp.where((before == rank2) & kept, heavy, 0.0)
+        heavy = jnp.where(before == rank2, heavy, 0.0)
         top = heavy.astype(BF16)
-        load[g, 0] = top
-        load[g, 1] = (heavy - top.astype(F32)).astype(BF16)
+        both = jnp.concatenate([top, (heavy - top.astype(F32)).astype(BF16)], axis=0)
+        load[g] = jnp.where(kept, mm(both, widen), 0.0).astype(BF16)
 
     source, inside = iota((256, 256), 1) // 16, iota((256, 256), 1) % 16
     target = (inside // 4) * 64 + ((inside // 2) % 2) * 32 + (source // 8) * 16 + (inside % 2) * 8 + source % 8
     order = one_hot(iota((256, 256), 0) == target).astype(BF16)
     wout_in.wait()
     for half in range(2):
+        wait_bytes(recv.at[pl.ds(64 * half, 64)], d_r.at[half])
+
         @pl.loop(0, 4)
         def _(i):
-            group = (mine + 8 - (4 * half + i)) % 8
-            wait_bytes(recv.at[pl.ds(group * 16, 16)], d_r.at[group])
-            got = mm(order, recv[pl.ds(group * 16, 16)].reshape(256, 512)).astype(BF16)
+            got = mm(order, recv[pl.ds(64 * half + i * 16, 16)].reshape(256, 512)).astype(BF16)
             to = pl.multiple_of(i * 32, 32)
             for j in range(4):
                 for e in range(2):
@@ -370,16 +407,15 @@
             rows = pl.ds(pl.multiple_of(e * 16, 16), 16)
             for f in range(HEADS):
                 got = mm(inner, wout[e, :, 256 * f : 256 * f + 256]).astype(BF16)
-                for i in range(4):
-                    group = (mine + 8 - (4 * half + i)) % 8
-                    for n in range(2):
-                        at = 32 * i + 16 * n
-                        back[group * 16 + n * 8 + f, rows, :] = got[at : at + 16]
-
-        @pl.loop(0, 4)
-        def _(i):
-            group = (mine + 8 - (4 * half + i)) % 8
-            spread(p, group * 16, back, home, b_s, b_r)
+                for i in range(8):
+                    back[64 * half + 8 * i + f, rows, :] = got[16 * i : 16 * i + 16]
+
+        for n in far_first(half):
+            batch, f = batch_at(n // 8, -1), head_at(n % 8, -1)
+            if n:
+                remote(back.at[n // 8 * 8 + f], home.at[p], b_s, b_r, (batch, f)).start()
+            else:
+                pltpu.make_async_copy(back.at[f], home.at[p], b_r).start()
 
         if half == 0:
             take(sp_recv, g_r)
@@ -397,10 +433,10 @@
     shared = mm(every, down[...])
     near = slices[:, 0].astype(F32).reshape(192, 256) + shared
     wait_bytes(home, b_r)
-    acc = jnp.zeros((192, 256), F32)
+    acc = jnp.zeros((384, 256), F32)
     for g in range(8):
-        got = home[16 * g : 16 * g + 16].reshape(512, 256)
-        acc = acc + mm(load[g, 0], got) + mm(load[g, 1], got)
+        acc = acc + mm(load[g], home[16 * g : 16 * g + 16].reshape(512, 256))
+    acc = acc[:192] + acc[192:]
     out = (near + acc.astype(BF16).astype(F32)).astype(BF16).reshape(HEADS, 3, 8, 256)
     for o in range(HEADS):
         out_ref[:, o] = out[o]
@@ -408,7 +444,8 @@
         copy.wait_send()
     take(ids_all, i_s)
     take(wts_all, w_s)
-    take(rs, rs_s)
+    wait_bytes(fs, f_s)
+    wait_bytes(rs, rs_s)
     take(psend, p_s)
     take(send, d_s)
     take(sp, g_s)
@@ -422,7 +459,7 @@
         layer_kernel,
         name="layer",
         out_shape=jax.ShapeDtypeStruct((3, HEADS, 8, 256), BF16),
-        in_specs=[VMEM] * 9 + [ANY] * 8,
+        in_specs=[VMEM] * 10 + [ANY] * 8,
         out_specs=VMEM,
         scratch_shapes=[
             pltpu.VMEM((HEADS, 3, 8, 2048), BF16),
@@ -443,14 +480,15 @@
             pltpu.VMEM((HEADS, 3, 8, 10), jnp.int32),
             pltpu.VMEM((HEADS, 3, 8, 10), F32),
             pltpu.VMEM((HEADS, 3, 8, 2048), BF16),
-            pltpu.VMEM((HEADS, 3, 8, 2048), BF16),
+            pltpu.VMEM((3, 3, 8, 2048), BF16),
+            pltpu.VMEM((4, 3, 8, 2048), BF16),
             pltpu.VMEM((DEVS, 16, 512), BF16),
             pltpu.VMEM((DEVS, 16, 512), BF16),
             pltpu.VMEM((HEADS, 2, 3, 8, 256), BF16),
             pltpu.VMEM((HEADS, 2, 3, 8, 256), BF16),
             pltpu.VMEM((128, 512), BF16),
             pltpu.VMEM((8, 256, 128), BF16),
-            pltpu.VMEM((8, 2, 192, 512), BF16),
+            pltpu.VMEM((8, 384, 512), BF16),
             pltpu.VMEM((2, 128, 2048), BF16),
             pltpu.VMEM((DEVS, 32, 256), BF16),
             pltpu.VMEM((DEVS, 32, 256), BF16),
@@ -459,8 +497,10 @@
             pltpu.VMEM((HEADS, 3, 8, 512), BF16),
             dma((7,)), dma((2,)), dma((7,)), dma((HEADS,)),
         ]
-        + [dma(())] * 9
-        + [dma((8,))]
+        + [dma(())] * 5
+        + [dma((3,))]
+        + [dma(())] * 5
+        + [dma((2,))]
         + [dma(())] * 6,
         compiler_params=pltpu.CompilerParams(
             collective_id=0, has_side_effects=True, vmem_limit_bytes=60 * 2**20
@@ -481,7 +521,8 @@
         routes.transpose(1, 0, 2),
         route_weight.transpose(1, 0, 2),
         norm_in.reshape(1, 2048),
-        jnp.stack([a_log, dt_bias]),
+        a_log.reshape(1, 2),
+        dt_bias.reshape(1, 2),
         norm_gate.reshape(1, 128),
         norm_post.reshape(1, 2048),
         w_ba.transpose(1, 2, 0),

time: 107 us -> 95.2 us (0.89)
  Pallas kernels: 102 us -> 92.3 us
  other arithmetic: 1.24 us -> 0 us
    pallas_call x1, Pallas kernels: 102 us -> 92.3 us  [layer(): pl.pallas_call(layer_kernel, name='layer', out_shape=jax.ShapeDtypeStruct...]
    another operation x1 -> x0, other arithmetic: 1.24 us -> none  [shards(): jnp.stack([a_log, dt_bias])]
where the time goes in v1:
time: 95.2 us; the launch traced here: 95 us
  Pallas kernels  92.3 us (97%)
  local copies, waits for them, and re-layouts  2.76 us (3%)
    pallas_call x1, Pallas kernels, layer(): pl.pallas_call(layer_kernel, name='layer', out_shape=jax.ShapeDtypeStruct...  92.3 us

profile of v1, /device:TPU:1, one launch (start us, length us, event | category | flops | bytes accessed | tf_op | source)
XLA Modules:
  0.0 95.0 jit_solution(12336776891128423707)
XLA Ops:
  0.0 1.2 %reshape.47.sgate_ref = bf16[1,256]{1,0:T(2,128)(2,1)} reshape(bf16[256]{0:T(256)(128)(2,1)} %param.30) | data formatting | bytes 1024 | tf_op jit(solution)/shard_map/reshape | solution.py:529
  1.2 92.3 %layer.1 = bf16[3,8,8,256]{3,2,1,0:T(8,128)(2,1)} custom-call(bf16[3,8,2048]{2,1,0:T(8,128)(2,1)} %bitcast.31, s32[3,8,10]{2,1,0:T(8,128)} %bitcast.33, f32[3,8,10]{2,1,0:T(8,128)} %bitcast.34, f32[1,2048]{1,0:T(1,128)} %bitcast.35, f32[1,2]{1,0:T(1,128)} %bitcast.37, f32[1,2]{1,0:T(1,128)} %bitcast.38, f32[1,128]{1,0:T(1,128)} %bitcast.39, ...), custom_call_target="tpu_custom_call" | custom-call | tf_op jit(solution)/shard_map/layer/pallas_call | solution.py:458
  93.5 1.5 %copy.22 = bf16[64,3,256]{2,0,1:T(8,128)(2,1)} copy(bf16[64,3,256]{2,0,1:T(8,128)(2,1)} %bitcast.30) | data formatting | bytes 196608

commit v2 on v1

--- a/solution.py
+++ b/solution.py
@@ -10,6 +10,8 @@
 HEADS = 8
 BATCH = 16
 DEVS = HEADS * BATCH
+CUTS = (0, 64, 128)
+PARTS = len(CUTS) - 1
 F32 = jnp.float32
 BF16 = jnp.bfloat16
 VMEM = pl.BlockSpec(memory_space=pltpu.VMEM)
@@ -63,12 +65,12 @@
     return dy, (place % 2) * 2 + (dy + place // 8) % 2
 
 
-def far_first(half):
+def far_first(part):
     def hops(position):
         dy, dz = plane_offset(position // 8)
         return sum(min(d, 4 - d) for d in (dy, dz, (position % 8) // 2))
 
-    return sorted(range(64 * half, 64 * half + 64), key=lambda position: (-hops(position), position % 5, position))
+    return sorted(range(CUTS[part], CUTS[part + 1]), key=lambda position: (-hops(position), position % 5, position))
 
 
 def part_rows(raw, wide, kinds, lane_of, blocks, from_row=0, to_row=0):
@@ -147,13 +149,13 @@
 
 
 def layer_kernel(
-    hid_ref, ids_ref, wt_ref, gain_in, alog_ref, dt_ref, gain_gate, gain_post, wba_ref, sgate_ref,
+    hid_hbm, ids_hbm, wt_hbm, gain_in_hbm, alog_hbm, dt_hbm, gain_gate_hbm, gain_post_hbm, wba_hbm, sgate_hbm,
     states_hbm, wqk_hbm, wvz_hbm, wo_hbm, sraw_hbm, down_hbm, win_hbm, wout_hbm,
     out_ref,
-    hall, nrm, proj, bas, states, wqk, wvz, wide, wo, sraw, swin, down, raw, win, wout,
+    hid_ref, ids_ref, wt_ref, gain_in, alog_ref, dt_ref, gain_gate, gain_post, wba_ref, sgate_ref, hall, nrm, proj, bas, states, wqk, wvz, wide, wo, sraw, swin, down, raw, win, wout,
     ids_all, wts_all, partb, fs, rs, send, recv, psend, slices, stacked, placing, load, xs,
     back, home, sp, sp_recv, mids,
-    in_sem, raw_sem, ag_s, ag_r, i_s, i_r, w_s, w_r, f_s, f_r, rs_s, rs_r, p_s, p_r, d_s, d_r, b_s, b_r, g_s, g_r, m_s, m_r,
+    small_sem, in_sem, raw_sem, ag_s, ag_r, i_s, i_r, w_s, w_r, f_s, f_r, rs_s, rs_r, p_s, p_r, d_s, d_r, b_s, b_r, g_s, g_r, m_s, m_r,
 ):
     b = lax.axis_index("batch")
     h = lax.axis_index("head")
@@ -186,6 +188,23 @@
             win_hbm.at[pl.ds(n * 8192, 8192)], raw.at[n % 2], raw_sem.at[n % 2]
         )
 
+    first = [
+        (hid_hbm, hid_ref), (ids_hbm, ids_ref), (wt_hbm, wt_ref), (gain_in_hbm, gain_in), (alog_hbm, alog_ref),
+        (dt_hbm, dt_ref), (gain_gate_hbm, gain_gate), (gain_post_hbm, gain_post), (wba_hbm, wba_ref),
+        (sgate_hbm, sgate_ref),
+    ]
+    first = [pltpu.make_async_copy(src, dst, small_sem.at[n]) for n, (src, dst) in enumerate(first)]
+    barrier = pltpu.get_barrier_semaphore()
+    for i in range(1, HEADS):
+        pl.semaphore_signal(barrier, inc=1, device_id=(b, (h + i) % HEADS), device_id_type=MESH)
+    for copy in first:
+        copy.start()
+
+    @pl.loop(1, BATCH)
+    def _(i):
+        for to in range(HEADS):
+            pl.semaphore_signal(barrier, inc=1, device_id=((b + i) % BATCH, to), device_id_type=MESH)
+
     for copy in loads[:4]:
         copy.start()
     raw_in(0).start()
@@ -193,12 +212,8 @@
     for copy in loads[4:]:
         copy.start()
 
-    barrier = pltpu.get_barrier_semaphore()
-
-    @pl.loop(1, DEVS)
-    def _(i):
-        pl.semaphore_signal(barrier, inc=1, device_id=spot((p + i) % DEVS), device_id_type=MESH)
-
+    for copy in first:
+        copy.wait()
     pl.semaphore_wait(barrier, DEVS - 1)
 
     sent = []
@@ -314,18 +329,18 @@
     to_heads(lambda to: psend.at[to], slices, p_s, p_r)
     slices[h] = psend[h]
 
-    for half in range(2):
-        @pl.loop(4 * half, 4 * half + 4)
+    for part in range(PARTS):
+        @pl.loop(CUTS[part] // 16, CUTS[part + 1] // 16)
         def _(g):
             rows = mm(placing[g], stacked[...]).astype(BF16)
             send[pl.ds(g * 16, 16)] = rows.reshape(16, 16, 512)
 
-        for n in far_first(half):
+        for n in far_first(part):
             if n:
                 to = (batch_at(n // 8, 1), head_at(n % 8, 1))
-                remote(send.at[n], recv.at[n], d_s, d_r.at[half], to).start()
+                remote(send.at[n], recv.at[n], d_s, d_r.at[part], to).start()
             else:
-                pltpu.make_async_copy(send.at[n], recv.at[n], d_r.at[half]).start()
+                pltpu.make_async_copy(send.at[n], recv.at[n], d_r.at[part]).start()
 
     def lay_out(n):
         raw_in(n).wait()
@@ -338,7 +353,8 @@
     take(slices, p_r)
     every = slices[:, 1].astype(F32).reshape(192, 256)
     up = mm(every.astype(BF16), swin[...])
-    logit = jnp.sum(every * sgate_ref[...].astype(F32), axis=-1, keepdims=True)
+    sgate = sgate_ref[...].astype(F32)
+    logit = jnp.sum(every[:, :128] * sgate[:1] + every[:, 128:] * sgate[1:], axis=-1, keepdims=True)
     high = logit.astype(BF16).astype(F32)
     zero = jnp.zeros((192, 126), F32)
     sp[...] = (
@@ -355,17 +371,19 @@
     wts = wts_all[...].reshape(192, 10)
     i0, i1 = iota((192, 192), 0), iota((192, 192), 1)
     later2 = one_hot((i0 // 24 == i1 // 24) & (i1 < i0)).astype(BF16)
-    named2 = iota((192, 64), 1) // 2
+    cell = iota((192, 64), 1)
+    named2 = head_at((cell // 4) % 8, 1) * 2 + (cell // 2) % 2
     rank2 = (iota((192, 64), 1) % 2).astype(F32)
     widen = one_hot(iota((64, 512), 1) // 8 == iota((64, 512), 0)).astype(BF16)
     col2 = iota((384, 512), 1)
-    source_head, member = (col2 // 32) % 8, col2 % 8
+    source_head, member = head_at((col2 // 32) % 8, 1), col2 % 8
     owner = ((source_head // 2 + 4 - member // 2) % 4) * 2 + (source_head + member) % 2
     kept = (iota((384, 512), 0) % 192) // 24 == owner
 
     @pl.loop(0, 8)
     def _(g):
-        here = named2 + g * 32
+        near, far = batch_at(2 * g, 1) * 16, batch_at(2 * g + 1, 1) * 16
+        here = named2 + jnp.where(cell < 32, near, far)
         hot = jnp.zeros((192, 64), F32)
         heavy = jnp.zeros((192, 64), F32)
         for k in range(10):
@@ -382,12 +400,13 @@
     target = (inside // 4) * 64 + ((inside // 2) % 2) * 32 + (source // 8) * 16 + (inside % 2) * 8 + source % 8
     order = one_hot(iota((256, 256), 0) == target).astype(BF16)
     wout_in.wait()
-    for half in range(2):
-        wait_bytes(recv.at[pl.ds(64 * half, 64)], d_r.at[half])
-
-        @pl.loop(0, 4)
+    for part in range(PARTS):
+        start, size = CUTS[part], CUTS[part + 1] - CUTS[part]
+        wait_bytes(recv.at[pl.ds(start, size)], d_r.at[part])
+
+        @pl.loop(0, size // 16)
         def _(i):
-            got = mm(order, recv[pl.ds(64 * half + i * 16, 16)].reshape(256, 512)).astype(BF16)
+            got = mm(order, recv[pl.ds(start + i * 16, 16)].reshape(256, 512)).astype(BF16)
             to = pl.multiple_of(i * 32, 32)
             for j in range(4):
                 for e in range(2):
@@ -400,24 +419,24 @@
             for n in range(2):
                 lane = slice(256 * n, 256 * n + 256)
                 lane2 = slice(512 + 256 * n, 768 + 256 * n)
-                gate = mm(xs[e], win[pl.ds(e * 2048, 2048), lane])
-                more = mm(xs[e], win[pl.ds(e * 2048, 2048), lane2])
+                gate = mm(xs[e, : 2 * size], win[pl.ds(e * 2048, 2048), lane])
+                more = mm(xs[e, : 2 * size], win[pl.ds(e * 2048, 2048), lane2])
                 inner.append((silu(gate) * more).astype(BF16))
             inner = jnp.concatenate(inner, axis=1)
             rows = pl.ds(pl.multiple_of(e * 16, 16), 16)
             for f in range(HEADS):
                 got = mm(inner, wout[e, :, 256 * f : 256 * f + 256]).astype(BF16)
-                for i in range(8):
-                    back[64 * half + 8 * i + f, rows, :] = got[16 * i : 16 * i + 16]
-
-        for n in far_first(half):
+                for i in range(size // 8):
+                    back[start + 8 * i + f, rows, :] = got[16 * i : 16 * i + 16]
+
+        for n in far_first(part):
             batch, f = batch_at(n // 8, -1), head_at(n % 8, -1)
             if n:
-                remote(back.at[n // 8 * 8 + f], home.at[p], b_s, b_r, (batch, f)).start()
+                remote(back.at[n // 8 * 8 + f], home.at[n], b_s, b_r.at[part], (batch, f)).start()
             else:
-                pltpu.make_async_copy(back.at[f], home.at[p], b_r).start()
-
-        if half == 0:
+                pltpu.make_async_copy(back.at[f], home.at[n], b_r.at[part]).start()
+
+        if part == 0:
             take(sp_recv, g_r)
             total = sp[h].astype(F32)
             for i in range(1, HEADS):
@@ -432,10 +451,12 @@
     every = mids[...].astype(F32).reshape(192, 512).astype(BF16)
     shared = mm(every, down[...])
     near = slices[:, 0].astype(F32).reshape(192, 256) + shared
-    wait_bytes(home, b_r)
     acc = jnp.zeros((384, 256), F32)
-    for g in range(8):
-        acc = acc + mm(load[g], home[16 * g : 16 * g + 16].reshape(512, 256))
+    for part in range(PARTS):
+        start, size = CUTS[part], CUTS[part + 1] - CUTS[part]
+        wait_bytes(home.at[pl.ds(start, size)], b_r.at[part])
+        for g in range(start // 16, (start + size) // 16):
+            acc = acc + mm(load[g], home[16 * g : 16 * g + 16].reshape(512, 256))
     acc = acc[:192] + acc[192:]
     out = (near + acc.astype(BF16).astype(F32)).astype(BF16).reshape(HEADS, 3, 8, 256)
     for o in range(HEADS):
@@ -459,9 +480,19 @@
         layer_kernel,
         name="layer",
         out_shape=jax.ShapeDtypeStruct((3, HEADS, 8, 256), BF16),
-        in_specs=[VMEM] * 10 + [ANY] * 8,
+        in_specs=[ANY] * 18,
         out_specs=VMEM,
         scratch_shapes=[
+            pltpu.VMEM((3, 8, 2048), BF16),
+            pltpu.VMEM((3, 8, 10), jnp.int32),
+            pltpu.VMEM((3, 8, 10), F32),
+            pltpu.VMEM((1, 2048), F32),
+            pltpu.VMEM((1, 2), F32),
+            pltpu.VMEM((1, 2), F32),
+            pltpu.VMEM((1, 128), F32),
+            pltpu.VMEM((1, 2048), F32),
+            pltpu.VMEM((2, 2, 2048), BF16),
+            pltpu.VMEM((2, 128), BF16),
             pltpu.VMEM((HEADS, 3, 8, 2048), BF16),
             pltpu.VMEM((192, 2048), F32),
             pltpu.VMEM((192, 768), F32),
@@ -489,19 +520,19 @@
             pltpu.VMEM((128, 512), BF16),
             pltpu.VMEM((8, 256, 128), BF16),
             pltpu.VMEM((8, 384, 512), BF16),
-            pltpu.VMEM((2, 128, 2048), BF16),
+            pltpu.VMEM((2, 2 * max(b - a for a, b in zip(CUTS, CUTS[1:])), 2048), BF16),
             pltpu.VMEM((DEVS, 32, 256), BF16),
             pltpu.VMEM((DEVS, 32, 256), BF16),
             pltpu.VMEM((HEADS, 3, 8, 1152), BF16),
             pltpu.VMEM((HEADS, 3, 8, 1152), BF16),
             pltpu.VMEM((HEADS, 3, 8, 512), BF16),
-            dma((7,)), dma((2,)), dma((7,)), dma((HEADS,)),
+            dma((10,)), dma((7,)), dma((2,)), dma((7,)), dma((HEADS,)),
         ]
         + [dma(())] * 5
         + [dma((3,))]
         + [dma(())] * 5
-        + [dma((2,))]
-        + [dma(())] * 6,
+        + [dma((PARTS,)), dma(()), dma((PARTS,))]
+        + [dma(())] * 4,
         compiler_params=pltpu.CompilerParams(
             collective_id=0, has_side_effects=True, vmem_limit_bytes=60 * 2**20
         ),
@@ -526,7 +557,7 @@
         norm_gate.reshape(1, 128),
         norm_post.reshape(1, 2048),
         w_ba.transpose(1, 2, 0),
-        shared_gate.reshape(1, 256),
+        shared_gate.reshape(2, 128),
         states,
         w_qk.reshape(4096, 128),
         w_vz.reshape(8192, 128),

time: 95.2 us -> 91.5 us (0.961)
  Pallas kernels: 92.3 us -> 89.8 us
  local copies, waits for them, and re-layouts: 2.76 us -> 1.54 us
    pallas_call x1, Pallas kernels: 92.3 us -> 89.8 us  [layer(): pl.pallas_call(layer_kernel, name='layer', out_shape=jax.ShapeDtypeStruct...]
    reshape x1 -> x0, local copies, waits for them, and re-layouts: 1.22 us -> none  [shards(): shared_gate.reshape(1, 256)]
where the time goes in v2:
time: 91.5 us; the launch traced here: 91.4 us
  Pallas kernels  89.8 us (98%)
  local copies, waits for them, and re-layouts  1.54 us (2%)
    pallas_call x1, Pallas kernels, layer(): pl.pallas_call(layer_kernel, name='layer', out_shape=jax.ShapeDtypeStruct...  89.8 us

profile of v2, /device:TPU:1, one launch (start us, length us, event | category | flops | bytes accessed | tf_op | source)
XLA Modules:
  0.0 91.4 jit_solution(486946663272222077)
XLA Ops:
  0.0 89.8 %layer.1 = bf16[3,8,8,256]{3,2,1,0:T(8,128)(2,1)} custom-call(bf16[3,8,2048]{2,1,0:T(8,128)(2,1)} %bitcast.32, s32[3,8,10]{2,1,0:T(8,128)} %bitcast.34, f32[3,8,10]{2,1,0:T(8,128)} %bitcast.35, f32[1,2048]{1,0:T(1,128)} %bitcast.36, f32[1,2]{1,0:T(1,128)} %bitcast.38, f32[1,2]{1,0:T(1,128)} %bitcast.39, f32[1,128]{1,0:T(1,128)} %bitcast.40, ...), custom_call_target="tpu_custom_call" | custom-call | tf_op jit(solution)/shard_map/layer/pallas_call | solution.py:479
  89.8 1.5 %copy.22 = bf16[64,3,256]{2,0,1:T(8,128)(2,1)} copy(bf16[64,3,256]{2,0,1:T(8,128)(2,1)} %bitcast.31) | data formatting | bytes 196608

commit v3 on v2

--- a/solution.py
+++ b/solution.py
@@ -266,24 +266,27 @@
     states_in.wait()
     wo_in.wait()
 
-    def partial_rows(o):
+    def gated_rows(o):
         at = pl.multiple_of(o * 24, 8)
-        gated = delta_rows(
+        return delta_rows(
             proj[pl.ds(at, 24)], bas[pl.ds(at, 24)], (alog_ref[...], dt_ref[...]), gain_gate[...],
             states[pl.ds(pl.multiple_of(o * 8, 8), 8)],
         )
-        gated = jnp.concatenate([gated, jnp.zeros((8, 256), F32)], axis=0).astype(BF16)
+
+    def partial_rows(o):
+        gated = jnp.concatenate([gated_rows(o), jnp.zeros((8, 256), F32)], axis=0).astype(BF16)
         return mm(gated, wo[...])[:24].reshape(3, 8, 2048)
+
+    others = [((x + d) % 4) * 2 + 1 - c for d in (2, 1, 3)]
+    gated = jnp.concatenate([gated_rows(o) for o in others] + [jnp.zeros((24, 256), F32)], axis=0)
+    rows = mm(gated.astype(BF16), wo[...])
+    for k, o in enumerate(others):
+        partb[o] = rows[24 * k : 24 * k + 24].reshape(3, 8, 2048).astype(BF16)
+        remote(partb.at[o], fs.at[k], f_s, f_r.at[k], (b, sib)).start()
 
     @pl.loop(0, 3)
     def _(k):
-        o = ((x + 1 + k) % 4) * 2 + 1 - c
-        partb[o] = partial_rows(o).astype(BF16)
-        remote(partb.at[o], fs.at[k], f_s, f_r.at[k], (b, sib)).start()
-
-    @pl.loop(0, 3)
-    def _(k):
-        o = ((x + 1 + k) % 4) * 2 + c
+        o = ((x + 2 - k + 3 * (k // 2)) % 4) * 2 + c
         rows = partial_rows(o)
         wait_bytes(fs.at[k], f_r.at[k])
         partb[o] = (rows + fs[k].astype(F32)).astype(BF16)
@@ -323,6 +326,7 @@
     stacked[...] = jnp.concatenate(
         [v for j in range(4) for v in (rows[:, 512 * j : 512 * j + 512], blank)], axis=0
     ).astype(BF16)
+
     for i in range(HEADS):
         psend[i, 0] = resid[:, :, 256 * i : 256 * i + 256]
         psend[i, 1] = post[:, :, 256 * i : 256 * i + 256]
@@ -341,6 +345,7 @@
                 remote(send.at[n], recv.at[n], d_s, d_r.at[part], to).start()
             else:
                 pltpu.make_async_copy(send.at[n], recv.at[n], d_r.at[part]).start()
+
 
     def lay_out(n):
         raw_in(n).wait()

time: 91.5 us -> 90.3 us (0.987)
  Pallas kernels: 89.8 us -> 88.6 us
    pallas_call x1, Pallas kernels: 89.8 us -> 88.6 us  [layer(): pl.pallas_call(layer_kernel, name='layer', out_shape=jax.ShapeDtypeStruct...]
where the time goes in v3:
time: 90.3 us; the launch traced here: 90.1 us
  Pallas kernels  88.6 us (98%)
  local copies, waits for them, and re-layouts  1.54 us (2%)
    pallas_call x1, Pallas kernels, layer(): pl.pallas_call(layer_kernel, name='layer', out_shape=jax.ShapeDtypeStruct...  88.6 us

profile of v3, /device:TPU:1, one launch (start us, length us, event | category | flops | bytes accessed | tf_op | source)
XLA Modules:
  0.0 90.1 jit_solution(16284403725047943102)
XLA Ops:
  0.0 88.6 %layer.1 = bf16[3,8,8,256]{3,2,1,0:T(8,128)(2,1)} custom-call(bf16[3,8,2048]{2,1,0:T(8,128)(2,1)} %bitcast.32, s32[3,8,10]{2,1,0:T(8,128)} %bitcast.34, f32[3,8,10]{2,1,0:T(8,128)} %bitcast.35, f32[1,2048]{1,0:T(1,128)} %bitcast.36, f32[1,2]{1,0:T(1,128)} %bitcast.38, f32[1,2]{1,0:T(1,128)} %bitcast.39, f32[1,128]{1,0:T(1,128)} %bitcast.40, ...), custom_call_target="tpu_custom_call" | custom-call | tf_op jit(solution)/shard_map/layer/pallas_call | solution.py:484
  88.6 1.5 %copy.22 = bf16[64,3,256]{2,0,1:T(8,128)(2,1)} copy(bf16[64,3,256]{2,0,1:T(8,128)(2,1)} %bitcast.31) | data formatting | bytes 196608

commit v4 on v3

--- a/solution.py
+++ b/solution.py
@@ -153,7 +153,7 @@
     states_hbm, wqk_hbm, wvz_hbm, wo_hbm, sraw_hbm, down_hbm, win_hbm, wout_hbm,
     out_ref,
     hid_ref, ids_ref, wt_ref, gain_in, alog_ref, dt_ref, gain_gate, gain_post, wba_ref, sgate_ref, hall, nrm, proj, bas, states, wqk, wvz, wide, wo, sraw, swin, down, raw, win, wout,
-    ids_all, wts_all, partb, fs, rs, send, recv, psend, slices, stacked, placing, load, xs,
+    ids_all, wts_all, partb, fs, rs, send, recv, psend, slices, stacked, placing, load, xs, inner,
     back, home, sp, sp_recv, mids,
     small_sem, in_sem, raw_sem, ag_s, ag_r, i_s, i_r, w_s, w_r, f_s, f_r, rs_s, rs_r, p_s, p_r, d_s, d_r, b_s, b_r, g_s, g_r, m_s, m_r,
 ):
@@ -420,26 +420,26 @@
 
         @pl.loop(0, 2)
         def _(e):
-            inner = []
             for n in range(2):
                 lane = slice(256 * n, 256 * n + 256)
                 lane2 = slice(512 + 256 * n, 768 + 256 * n)
                 gate = mm(xs[e, : 2 * size], win[pl.ds(e * 2048, 2048), lane])
                 more = mm(xs[e, : 2 * size], win[pl.ds(e * 2048, 2048), lane2])
-                inner.append((silu(gate) * more).astype(BF16))
-            inner = jnp.concatenate(inner, axis=1)
-            rows = pl.ds(pl.multiple_of(e * 16, 16), 16)
-            for f in range(HEADS):
-                got = mm(inner, wout[e, :, 256 * f : 256 * f + 256]).astype(BF16)
+                inner[e, : 2 * size, lane] = (silu(gate) * more).astype(BF16)
+
+        for member in (4, 5, 2, 3, 6, 7, 0, 1):
+            f = head_at(member, -1)
+            lane = pl.ds(pl.multiple_of(f * 256, 256), 256)
+            for e in range(2):
+                got = mm(inner[e, : 2 * size], wout[e, :, lane]).astype(BF16)
                 for i in range(size // 8):
-                    back[start + 8 * i + f, rows, :] = got[16 * i : 16 * i + 16]
-
-        for n in far_first(part):
-            batch, f = batch_at(n // 8, -1), head_at(n % 8, -1)
-            if n:
-                remote(back.at[n // 8 * 8 + f], home.at[n], b_s, b_r.at[part], (batch, f)).start()
-            else:
-                pltpu.make_async_copy(back.at[f], home.at[n], b_r.at[part]).start()
+                    back[start + 8 * i + member, 16 * e : 16 * e + 16, :] = got[16 * i : 16 * i + 16]
+            for n in far_first(part):
+                if n % 8 == member:
+                    if n:
+                        remote(back.at[n], home.at[n], b_s, b_r.at[part], (batch_at(n // 8, -1), f)).start()
+                    else:
+                        pltpu.make_async_copy(back.at[n], home.at[n], b_r.at[part]).start()
 
         if part == 0:
             take(sp_recv, g_r)
@@ -526,6 +526,7 @@
             pltpu.VMEM((8, 256, 128), BF16),
             pltpu.VMEM((8, 384, 512), BF16),
             pltpu.VMEM((2, 2 * max(b - a for a, b in zip(CUTS, CUTS[1:])), 2048), BF16),
+            pltpu.VMEM((2, 2 * max(b - a for a, b in zip(CUTS, CUTS[1:])), 512), BF16),
             pltpu.VMEM((DEVS, 32, 256), BF16),
             pltpu.VMEM((DEVS, 32, 256), BF16),
             pltpu.VMEM((HEADS, 3, 8, 1152), BF16),
@@ -539,7 +540,7 @@
         + [dma((PARTS,)), dma(()), dma((PARTS,))]
         + [dma(())] * 4,
         compiler_params=pltpu.CompilerParams(
-            collective_id=0, has_side_effects=True, vmem_limit_bytes=60 * 2**20
+            collective_id=0, has_side_effects=True, vmem_limit_bytes=55 * 2**20
         ),
     )(*args)
 

time: 90.3 us -> 90.5 us (level)
  no operation moved by 1% of the time
where the time goes in v4:
time: 90.5 us; the launch traced here: 90.3 us
  Pallas kernels  88.8 us (98%)
  local copies, waits for them, and re-layouts  1.54 us (2%)
    pallas_call x1, Pallas kernels, layer(): pl.pallas_call(layer_kernel, name='layer', out_shape=jax.ShapeDtypeStruct...  88.8 us

profile of v4, /device:TPU:1, one launch (start us, length us, event | category | flops | bytes accessed | tf_op | source)
XLA Modules:
  0.0 90.3 jit_solution(14879693723338195420)
XLA Ops:
  0.0 88.8 %layer.1 = bf16[3,8,8,256]{3,2,1,0:T(8,128)(2,1)} custom-call(bf16[3,8,2048]{2,1,0:T(8,128)(2,1)} %bitcast.32, s32[3,8,10]{2,1,0:T(8,128)} %bitcast.34, f32[3,8,10]{2,1,0:T(8,128)} %bitcast.35, f32[1,2048]{1,0:T(1,128)} %bitcast.36, f32[1,2]{1,0:T(1,128)} %bitcast.38, f32[1,2]{1,0:T(1,128)} %bitcast.39, f32[1,128]{1,0:T(1,128)} %bitcast.40, ...), custom_call_target="tpu_custom_call" | custom-call | tf_op jit(solution)/shard_map/layer/pallas_call | solution.py:484
  88.8 1.5 %copy.22 = bf16[64,3,256]{2,0,1:T(8,128)(2,1)} copy(bf16[64,3,256]{2,0,1:T(8,128)(2,1)} %bitcast.31) | data formatting | bytes 196608
